TPU v7x, 32 devices: a whole 2x2x4 slice. The times are simulated.
32 devices in a mesh: grp: 2 (over x), row: 16 (over z, y, core).
Axes of the slice: x: 2, y: 2, z: 4, core: 2. Of those that a mesh axis runs over, the one named last changes fastest.
Arguments:
- geometry: float32 [9, 16384], P(None, ('grp', 'row')), parts along dimension 1, as said below
- emission: float32 [16, 16384], P(None, ('grp', 'row')), parts along dimension 1, may hold values from 0.1 to 10
- reflect: float32 [16384], P(('grp', 'row')), parts along dimension 0, may hold values from 0.2 to 0.8
- occlusion: int32 [1024, 256], P(('grp', 'row')), parts along dimension 0, may hold values from 0 to 65535
- pair_recv: int32 [1024], P(('grp', 'row')), parts along dimension 0, may hold values from 0 to 31, as said below
- pair_src: int32 [1024], P(('grp', 'row')), parts along dimension 0, may hold values from 0 to 1
- pair_count: int32 [32], P(('grp', 'row')), parts along dimension 0, may hold values from 8 to 32, as said below
Outputs:
- radiosity: float32 [16, 16384], P(None, ('grp', 'row')), parts along dimension 1
- row_sums: float32 [16384], P(('grp', 'row')), parts along dimension 0
There are 2 independent parts, one for each index of `grp`. A program takes and returns all parts, laid end to end along the dimension named above; each array names one. Nothing has to cross between parts.
Inputs may be any that keep to these rules, and one draw needn't show every extreme that they name: `pair_recv`: in each index of row the 32 slots name distinct receiving tiles. `pair_count`: some index of row has all 32 slots live in every draw. `geometry`: edges are never parallel; every area is 0.2 or more.
All inputs are finite; a program needn't handle non-finite values.
Results may differ from a plain program's by a relative error of at most 0.0003.
Values sent between devices are 32-bit elements; how exact they have to be, the bound alone decides.
A program may use at most 64 MiB of HBM per device.

v0:
```python
import functools
import math

import jax
import jax.numpy as jnp
from jax import lax
from jax.experimental import pallas as pl
from jax.experimental.pallas import tpu as pltpu
from jax.sharding import PartitionSpec as P

TILE = 256
GROUPS = 16
BAND = TILE // GROUPS
POINTS = 4
FEATS = 48
PACK = 32
CHUNKS = 4
PART = TILE // CHUNKS
SPAN = (POINTS + 1) * TILE
VMEM = pl.BlockSpec(memory_space=pltpu.VMEM)
SMEM = pl.BlockSpec(memory_space=pltpu.SMEM)


def sort_kernel(recv_ref, src_ref, count_ref, occ_ref, table_ref):
    tiles = table_ref.shape[0]
    table_ref[:, :, :TILE] = jnp.zeros((tiles, 1, TILE), jnp.int32)
    table_ref[:, :, TILE:] = jnp.full((tiles, 1, 128), -1, jnp.int32)

    def place(k, carry):
        row = recv_ref[k]
        table_ref[row, :, :TILE] = occ_ref[pl.ds(k, 1), :]
        table_ref[row, :, TILE:] = jnp.full((1, 128), src_ref[k], jnp.int32)
        return carry

    lax.fori_loop(0, count_ref[0], place, 0)


def start_gather(n, own, out, send, recv):
    me = lax.axis_index("row")
    depth = n // 4
    core = lax.rem(me, 2)
    side = lax.rem(me // 2, 2)
    level = me // 4

    def index(a, b, c):
        return a * 4 + b * 2 + c

    def copy(source, slot, device, k):
        return pltpu.make_async_remote_copy(
            src_ref=source,
            dst_ref=out.at[slot],
            send_sem=send.at[k],
            recv_sem=recv.at[slot],
            device_id={"row": device},
            device_id_type=pl.DeviceIdType.MESH,
        )

    across = index(level, 1 - side, core)
    partner = index(level, side, 1 - core)
    started = []

    def begin(source, slot, device):
        made = copy(source, slot, device, len(started))
        made.start()
        started.append(made)

    for step in range(1, depth):
        begin(own, me, index(lax.rem(level + step, depth), side, core))
    begin(own, me, across)
    begin(own, me, partner)

    def arrived(slot):
        copy(out.at[slot], slot, partner, 0).wait_recv()

    def finish():
        for step in range(1, depth):
            slot = index(lax.rem(level - step + depth, depth), side, core)
            arrived(slot)
            begin(out.at[slot], slot, across)
            begin(out.at[slot], slot, partner)
        for step in range(depth):
            slot = index(lax.rem(level - step + depth, depth), 1 - side, core)
            arrived(slot)
            begin(out.at[slot], slot, partner)
        for step in range(depth):
            for b in range(2):
                arrived(index(lax.rem(level - step + depth, depth), b, 1 - core))
        for made in started:
            made.wait_send()

    return finish


def sends(n):
    depth = n // 4
    return 3 * depth - 1 + 2 * depth


def greet(n):
    me = lax.axis_index("row")
    barrier = pltpu.get_barrier_semaphore()
    for step in range(1, n):
        pl.semaphore_signal(
            barrier,
            inc=1,
            device_id={"row": lax.rem(me + step, n)},
            device_id_type=pl.DeviceIdType.MESH,
        )
    pl.semaphore_wait(barrier, n - 1)


def share_kernel(n, emi_ref, geo_ref, table_ref, out_ref, listed_ref, codes_ref, send, recv, list_send, list_recv):
    me = lax.axis_index("row")
    hours = emi_ref.shape[0]
    own_tiles = table_ref.shape[0] // n
    out_ref[me, :hours] = emi_ref[...]
    out_ref[me, hours : hours + 9] = geo_ref[...]
    out_ref[me, hours + 9 :] = jnp.zeros_like(out_ref[me, hours + 9 :])
    listed_ref[me] = table_ref[pl.ds(me * own_tiles, own_tiles)]
    greet(n)
    finish = start_gather(n, out_ref.at[me], out_ref, send, recv)
    lists = []
    for step in range(1, n):
        device = lax.rem(me + step, n)
        made = pltpu.make_async_remote_copy(
            src_ref=table_ref.at[pl.ds(device * own_tiles, own_tiles)],
            dst_ref=listed_ref.at[me],
            send_sem=list_send.at[step],
            recv_sem=list_recv.at[step],
            device_id={"row": device},
            device_id_type=pl.DeviceIdType.MESH,
        )
        made.start()
        lists.append(made)
    finish()
    for made in lists:
        made.wait()
    for d in range(n):
        codes_ref[d * own_tiles : (d + 1) * own_tiles, :] = listed_ref[d, :, 0, TILE:]


def field_kernel(n, field_ref, out_ref, send, recv):
    me = lax.axis_index("row")
    out_ref[me] = field_ref[...]
    greet(n)
    start_gather(n, field_ref, out_ref, send, recv)()


def split3(x):
    high = x.astype(jnp.bfloat16).astype(jnp.float32)
    rest = x - high
    mid = rest.astype(jnp.bfloat16).astype(jnp.float32)
    return high, mid, rest - mid


def split2(x):
    high = x.astype(jnp.bfloat16)
    return high, (x - high.astype(jnp.float32)).astype(jnp.bfloat16)


def frame(geo, center):
    corner = geo[0:3] - center
    u = geo[3:6]
    v = geo[6:9]
    ux, uy, uz = u[0:1], u[1:2], u[2:3]
    vx, vy, vz = v[0:1], v[1:2], v[2:3]
    cross = jnp.concatenate([uy * vz - uz * vy, uz * vx - ux * vz, ux * vy - uy * vx], axis=0)
    area = jnp.sqrt(jnp.sum(cross * cross, axis=0, keepdims=True))
    points = jnp.concatenate(
        [corner + s * u + t * v for s in (0.25, 0.75) for t in (0.25, 0.75)], axis=1
    )
    return points, corner, cross, area


def receiver_features(geo, center):
    points, corner, cross, area = frame(geo, center)
    normal = cross / area
    norms = jnp.sum(points * points, axis=0, keepdims=True)
    offset = -jnp.sum(normal * corner, axis=0, keepdims=True)
    wide = jnp.concatenate([-2.0 * points, normal], axis=1)
    fourth = jnp.concatenate([jnp.ones_like(norms), jnp.zeros_like(offset)], axis=1)
    fifth = jnp.concatenate([norms, offset], axis=1)
    rows = jnp.concatenate([wide, fourth, fifth, jnp.zeros((3, SPAN), jnp.float32)], axis=0)
    h, m, l = split3(rows)
    return jnp.concatenate([h, m, l, h, m, h], axis=0).astype(jnp.bfloat16)


def source_features(geo, center):
    points, corner, cross, area = frame(geo, center)
    scaled = cross * (1.0 / (16.0 * math.pi))
    norms = jnp.sum(points * points, axis=0, keepdims=True)
    spread = norms + jnp.concatenate([area * 0.25] * POINTS, axis=1)
    offset = -jnp.sum(scaled * corner, axis=0, keepdims=True)
    wide = jnp.concatenate([points, -0.5 * scaled], axis=1)
    fourth = jnp.concatenate([spread, offset], axis=1)
    fifth = jnp.concatenate([jnp.ones_like(norms), jnp.zeros_like(offset)], axis=1)
    rows = jnp.concatenate([wide, fourth, fifth, jnp.zeros((3, SPAN), jnp.float32)], axis=0)
    h, m, l = split3(rows)
    return jnp.concatenate([h, h, h, m, m, l], axis=0).T.astype(jnp.bfloat16)


def first_kernel(
    src_ref, packed, occ_ref, geo_own, emi_own, refl_ref,
    blocks_ref, field_ref, sums_ref, scale_ref,
    order, recv_feat, src_feat, dots, facing, total, acc,
):
    own_tiles = geo_own.shape[1] // TILE
    slots = packed.shape[0] * own_tiles
    hours = emi_own.shape[0]
    center = jnp.mean(geo_own[0:3, :], axis=1, keepdims=True)

    def listing(k, live):
        order[live] = k
        return live + jnp.where(src_ref[k, 0] >= 0, 1, 0)

    count = lax.fori_loop(0, slots, listing, 0)
    for r in range(own_tiles):
        recv_feat[r] = receiver_features(geo_own[:, r * TILE : (r + 1) * TILE], center)
    acc[...] = jnp.zeros_like(acc)

    def place(slot):
        src = jnp.maximum(src_ref[slot, 0], 0)
        return slot // own_tiles, pl.ds(pl.multiple_of(src * TILE, TILE), TILE)

    def load_features(slot):
        d, where = place(slot)
        rows = source_features(packed[d, hours : hours + 9, where], center)
        for c in range(CHUNKS):
            for q in range(POINTS):
                src_feat[c * TILE + q * PART : c * TILE + (q + 1) * PART, :] = rows[
                    q * TILE + c * PART : q * TILE + (c + 1) * PART
                ]
        src_feat[POINTS * TILE :, :] = rows[POINTS * TILE :]

    def product(r, piece, p):
        return jnp.dot(
            src_feat[piece * TILE : (piece + 1) * TILE, :],
            recv_feat[r, :, p * TILE : (p + 1) * TILE],
            preferred_element_type=jnp.float32,
        )

    def face(r, c):
        facing[c * TILE : (c + 1) * TILE, :] = jnp.maximum(product(r, c, POINTS), 0.0)

    def fill(r, c, p):
        dots[p % 2, c * TILE : (c + 1) * TILE, :] = product(r, c, p)

    def combine(p, c, finish):
        for b in range(PART // BAND):
            inner = b * BAND
            part = jnp.zeros((BAND, TILE), jnp.float32)
            for q in range(POINTS):
                row = c * TILE + q * PART + inner
                spread = dots[p % 2, row : row + BAND, :]
                inverse = pl.reciprocal(spread * spread, approx=True)
                part += facing[row : row + BAND, :] * inverse
            row = c * PART + inner
            back = dots[p % 2, POINTS * TILE + row : POINTS * TILE + row + BAND, :]
            value = jnp.maximum(back, 0.0) * part
            if p > 0:
                value += total[row : row + BAND, :]
            if p < POINTS - 1:
                total[row : row + BAND, :] = value
            else:
                finish(row, value)

    def prepare(slot):
        load_features(slot)
        r = lax.rem(slot, own_tiles)
        fill(r, CHUNKS, 0)
        for c in range(CHUNKS):
            face(r, c)
            fill(r, c, 0)

    prepare(order[0])

    def one(i, carry):
        slot = order[i]
        later = order[jnp.minimum(i + 1, count - 1)]
        r = lax.rem(slot, own_tiles)
        later_r = lax.rem(later, own_tiles)
        d, where = place(slot)
        words = occ_ref[d, r, :, :TILE]

        def finish(row, value):
            bit = jnp.bitwise_and(jnp.right_shift(words, row // BAND), 1).astype(jnp.float32)
            high, low = split2(value * bit)
            blocks_ref[slot, row : row + BAND, :] = high
            blocks_ref[slot, TILE + row : TILE + row + BAND, :] = low

        for p in range(POINTS - 1):
            fill(r, CHUNKS, p + 1)
            for c in range(CHUNKS):
                fill(r, c, p + 1)
                combine(p, c, finish)
        load_features(later)
        fill(later_r, CHUNKS, 0)
        for c in range(CHUNKS):
            combine(POINTS - 1, c, finish)
            face(later_r, c)
            fill(later_r, c, 0)
        high, low = split2(packed[d, :hours, where])
        left = jnp.concatenate([high, low, jnp.ones_like(high)], axis=0)
        acc[r] += jnp.dot(
            jnp.concatenate([left, left], axis=1),
            blocks_ref[slot],
            preferred_element_type=jnp.float32,
        )
        return carry

    lax.fori_loop(0, count, one, 0)
    for r in range(own_tiles):
        lanes = slice(r * TILE, (r + 1) * TILE)
        sums = acc[r, 2 * hours : 2 * hours + 1, :]
        irr = acc[r, 0:hours, :] + acc[r, hours : 2 * hours, :]
        scale = refl_ref[:, lanes] / jnp.maximum(sums, 1.0)
        sums_ref[:, lanes] = sums
        scale_ref[:, lanes] = scale
        field_ref[:, lanes] = emi_own[:, lanes] + scale * irr


def later_kernel(src_ref, blocks_ref, field_all, emi_own, scale_ref, out_ref, acc):
    slots = field_all.shape[0]
    own_tiles = emi_own.shape[1] // TILE
    hours = emi_own.shape[0]
    for r in range(own_tiles):
        lanes = slice(r * TILE, (r + 1) * TILE)
        acc[...] = jnp.zeros_like(acc)

        def one(d, carry):
            slot = d * own_tiles + r
            src = src_ref[slot, 0]

            @pl.when(src >= 0)
            def _():
                where = pl.ds(pl.multiple_of(src * TILE, TILE), TILE)
                high, low = split2(field_all[d, :, where])
                left = jnp.concatenate([high, low], axis=0)
                acc[...] += jnp.dot(
                    jnp.concatenate([left, left], axis=1),
                    blocks_ref[slot],
                    preferred_element_type=jnp.float32,
                )

            return carry

        lax.fori_loop(0, slots, one, 0)
        irr = acc[0:hours, :] + acc[hours : 2 * hours, :]
        out_ref[:, lanes] = emi_own[:, lanes] + scale_ref[:, lanes] * irr


def on_device(n, geometry, emission, reflect, occlusion, pair_recv, pair_src, pair_count):
    width = geometry.shape[1]
    hours = emission.shape[0]
    own_tiles = width // TILE
    tiles = own_tiles * n
    f32 = jnp.float32
    limit = pltpu.CompilerParams(vmem_limit_bytes=60 * 1024 * 1024)

    table = pl.pallas_call(
        sort_kernel,
        out_shape=jax.ShapeDtypeStruct((tiles, 1, TILE + 128), jnp.int32),
        in_specs=[SMEM, SMEM, SMEM, VMEM],
        out_specs=VMEM,
    )(pair_recv, pair_src, pair_count, occlusion)
    dma = pltpu.SemaphoreType.DMA
    packed, listed, codes = pl.pallas_call(
        functools.partial(share_kernel, n),
        out_shape=(
            jax.ShapeDtypeStruct((n, PACK, width), f32),
            jax.ShapeDtypeStruct((n, own_tiles, 1, TILE + 128), jnp.int32),
            jax.ShapeDtypeStruct((tiles, 128), jnp.int32),
        ),
        in_specs=[VMEM] * 3,
        out_specs=(VMEM,) * 3,
        scratch_shapes=[dma((sends(n),)), dma((n,)), dma((n,)), dma((n,))],
        compiler_params=pltpu.CompilerParams(
            collective_id=0, has_side_effects=True, vmem_limit_bytes=60 * 1024 * 1024
        ),
    )(emission, geometry, table)

    blocks, field, sums, scale = pl.pallas_call(
        first_kernel,
        out_shape=(
            jax.ShapeDtypeStruct((tiles, 2 * TILE, TILE), jnp.bfloat16),
            jax.ShapeDtypeStruct((hours, width), f32),
            jax.ShapeDtypeStruct((1, width), f32),
            jax.ShapeDtypeStruct((1, width), f32),
        ),
        in_specs=[SMEM] + [VMEM] * 5,
        out_specs=(VMEM,) * 4,
        scratch_shapes=[
            pltpu.SMEM((tiles,), jnp.int32),
            pltpu.VMEM((own_tiles, FEATS, SPAN), jnp.bfloat16),
            pltpu.VMEM((SPAN, FEATS), jnp.bfloat16),
            pltpu.VMEM((2, SPAN, TILE), f32),
            pltpu.VMEM((POINTS * TILE, TILE), f32),
            pltpu.VMEM((TILE, TILE), f32),
            pltpu.VMEM((own_tiles, 3 * hours, TILE), f32),
        ],
        compiler_params=limit,
    )(codes, packed, listed, geometry, emission, reflect.reshape(1, width))

    field_all = pl.pallas_call(
        functools.partial(field_kernel, n),
        out_shape=jax.ShapeDtypeStruct((n, hours, width), f32),
        in_specs=[VMEM],
        out_specs=VMEM,
        scratch_shapes=[dma((sends(n),)), dma((n,))],
        compiler_params=pltpu.CompilerParams(
            collective_id=1, has_side_effects=True, vmem_limit_bytes=60 * 1024 * 1024
        ),
    )(field)
    radiosity = pl.pallas_call(
        later_kernel,
        out_shape=jax.ShapeDtypeStruct((hours, width), f32),
        in_specs=[SMEM] + [VMEM] * 4,
        out_specs=VMEM,
        scratch_shapes=[pltpu.VMEM((2 * hours, TILE), f32)],
        compiler_params=limit,
    )(codes, blocks, field_all, emission, scale)
    return (radiosity, sums.reshape(width))


def solution(mesh):
    placed = (
        P(None, ("grp", "row")),
        P(None, ("grp", "row")),
        P(("grp", "row")),
        P(("grp", "row"), None),
        P(("grp", "row")),
        P(("grp", "row")),
        P(("grp", "row")),
    )
    return jax.shard_map(
        functools.partial(on_device, mesh.shape["row"]),
        mesh=mesh,
        in_specs=placed,
        out_specs=(P(None, ("grp", "row")), P(("grp", "row"))),
        check_vma=False,
    )
```

profile of v0, /device:TPU:1, one launch (start us, length us, event | category | flops | bytes accessed | tf_op | source)
XLA Modules:
  0.0 70.4 jit_solution(17953144109365710632)
XLA Ops:
  1.3 1.5 %shard_map.86.table_ref = s32[32,1,384]{2,1,0:T(1,128)} custom-call(s32[32]{0:T(128)} %recv_ref.1, s32[32]{0:T(128)} %src_ref.1, s32[1]{0:T(128)S(6)} %copy.9.count_ref, s32[32,256]{1,0:T(8,128)} %occ_ref.1), custom_call_target="tpu_custom_call" | custom-call | tf_op jit(solution)/shard_map/pallas_call | solution.py:360
  2.8 19.9 %shard_map.87 = (f32[16,32,512]{2,1,0:T(8,128)}, s32[16,2,1,384]{3,2,1,0:T(1,128)}, s32[32,128]{1,0:T(8,128)}) custom-call(f32[16,512]{1,0:T(8,128)} %emi_own.3, f32[9,512]{1,0:T(8,128)} %geo_own.1, s32[32,1,384]{2,1,0:T(1,128)} %shard_map.86.table_ref), custom_call_target="tpu_custom_call" | custom-call | tf_op jit(solution)/shard_map/pallas_call | solution.py:367
  22.6 23.9 %shard_map.88 = (bf16[32,512,256]{2,1,0:T(8,128)(2,1)}, f32[16,512]{1,0:T(8,128)}, f32[1,512]{1,0:T(1,128)}, f32[1,512]{1,0:T(1,128)}) custom-call(s32[32,128]{1,0:T(8,128)} %get-tuple-element.9.src_ref, f32[16,32,512]{2,1,0:T(8,128)} %get-tuple-element.10.packed, s32[16,2,1,384]{3,2,1,0:T(1,128)} %get-tuple-element.11.occ_ref, f32[9,512]{1,0:T(8,128)} %geo_own.1, ...), custom_call_target="tpu_custom_call" | custom-call | tf_op jit(solution)/shard_map/pallas_call | solution.py:382
  46.6 17.2 %shard_map.89.field_all = f32[16,16,512]{2,1,0:T(8,128)} custom-call(f32[16,512]{1,0:T(8,128)} %get-tuple-element.13.field_ref), custom_call_target="tpu_custom_call" | custom-call | tf_op jit(solution)/shard_map/pallas_call | solution.py:404
  63.8 6.6 %shard_map.90 = f32[16,512]{1,0:T(8,128)} custom-call(s32[32,128]{1,0:T(8,128)} %get-tuple-element.9.src_ref, bf16[32,512,256]{2,1,0:T(8,128)(2,1)} %get-tuple-element.12.blocks_ref, f32[16,16,512]{2,1,0:T(8,128)} %shard_map.89.field_all, f32[16,512]{1,0:T(8,128)} %emi_own.3, f32[1,512]{1,0:T(1,128)} %get-tuple-element.14.scale_ref), custom_call_target="tpu_custom_call" | custom-call | tf_op jit(solution)/shard_map/pallas_call | solution.py:414
where the time goes:
time: 69.6 us; the launch traced here: 70.4 us
  Pallas kernels  69.1 us (99%)
  between operations  1.29 us (2%)
    pallas_call x1, Pallas kernels, on_device(): pl.pallas_call(first_kernel, out_shape=(jax.ShapeDtypeStruct((tiles, 2 *...  23.9 us
    pallas_call x1, Pallas kernels, on_device(): pl.pallas_call(functools.partial(share_kernel, n), out_shape=(jax.ShapeDt...  19.9 us
    pallas_call x1, Pallas kernels, on_device(): pl.pallas_call(functools.partial(field_kernel, n), out_shape=jax.ShapeDty...  17.2 us
    pallas_call x1, Pallas kernels, on_device(): pl.pallas_call(later_kernel, out_shape=jax.ShapeDtypeStruct((hours, width...  6.6 us
    pallas_call x1, Pallas kernels, on_device(): pl.pallas_call(sort_kernel, out_shape=jax.ShapeDtypeStruct((tiles, 1, TIL...  1.5 us

commit v1 on v0

--- a/solution.py
+++ b/solution.py
@@ -16,8 +16,10 @@
 PACK = 32
 CHUNKS = 4
 PART = TILE // CHUNKS
+WIDE = 2 * TILE
 SPAN = (POINTS + 1) * TILE
 VMEM = pl.BlockSpec(memory_space=pltpu.VMEM)
+ANY = pl.BlockSpec(memory_space=pl.ANY)
 SMEM = pl.BlockSpec(memory_space=pltpu.SMEM)
 
 
@@ -202,7 +204,7 @@
 def first_kernel(
     src_ref, packed, occ_ref, geo_own, emi_own, refl_ref,
     blocks_ref, field_ref, sums_ref, scale_ref,
-    order, recv_feat, src_feat, dots, facing, total, acc,
+    order, recv_feat, src_feat, dots, facing, total, acc, block, sent,
 ):
     own_tiles = geo_own.shape[1] // TILE
     slots = packed.shape[0] * own_tiles
@@ -232,37 +234,42 @@
                 ]
         src_feat[POINTS * TILE :, :] = rows[POINTS * TILE :]
 
-    def product(r, piece, p):
+    def product(r, piece, start, wide):
         return jnp.dot(
             src_feat[piece * TILE : (piece + 1) * TILE, :],
-            recv_feat[r, :, p * TILE : (p + 1) * TILE],
+            recv_feat[r, :, start : start + wide],
             preferred_element_type=jnp.float32,
         )
 
     def face(r, c):
-        facing[c * TILE : (c + 1) * TILE, :] = jnp.maximum(product(r, c, POINTS), 0.0)
-
-    def fill(r, c, p):
-        dots[p % 2, c * TILE : (c + 1) * TILE, :] = product(r, c, p)
-
-    def combine(p, c, finish):
+        facing[c * TILE : (c + 1) * TILE, :] = jnp.maximum(
+            product(r, c, POINTS * TILE, TILE), 0.0
+        )
+
+    def fill(r, c, half):
+        dots[half, c * TILE : (c + 1) * TILE, :] = product(r, c, half * WIDE, WIDE)
+
+    def combine(half, c, finish):
         for b in range(PART // BAND):
             inner = b * BAND
-            part = jnp.zeros((BAND, TILE), jnp.float32)
+            parts = [jnp.zeros((BAND, TILE), jnp.float32) for _ in range(WIDE // TILE)]
             for q in range(POINTS):
                 row = c * TILE + q * PART + inner
-                spread = dots[p % 2, row : row + BAND, :]
-                inverse = pl.reciprocal(spread * spread, approx=True)
-                part += facing[row : row + BAND, :] * inverse
+                ahead = facing[row : row + BAND, :]
+                for k in range(WIDE // TILE):
+                    spread = dots[half, row : row + BAND, k * TILE : (k + 1) * TILE]
+                    parts[k] += ahead * pl.reciprocal(spread * spread, approx=True)
             row = c * PART + inner
-            back = dots[p % 2, POINTS * TILE + row : POINTS * TILE + row + BAND, :]
-            value = jnp.maximum(back, 0.0) * part
-            if p > 0:
-                value += total[row : row + BAND, :]
-            if p < POINTS - 1:
+            value = None
+            for k in range(WIDE // TILE):
+                start = POINTS * TILE + row
+                back = dots[half, start : start + BAND, k * TILE : (k + 1) * TILE]
+                term = jnp.maximum(back, 0.0) * parts[k]
+                value = term if value is None else value + term
+            if half == 0:
                 total[row : row + BAND, :] = value
             else:
-                finish(row, value)
+                finish(row, total[row : row + BAND, :] + value)
 
     def prepare(slot):
         load_features(slot)
@@ -272,6 +279,9 @@
             face(r, c)
             fill(r, c, 0)
 
+    def stored(slot, spot):
+        return pltpu.make_async_copy(block.at[spot], blocks_ref.at[slot], sent.at[spot])
+
     prepare(order[0])
 
     def one(i, carry):
@@ -281,34 +291,45 @@
         later_r = lax.rem(later, own_tiles)
         d, where = place(slot)
         words = occ_ref[d, r, :, :TILE]
+        spot = lax.rem(i, 2)
+
+        @pl.when(i >= 2)
+        def _():
+            stored(slot, spot).wait()
 
         def finish(row, value):
             bit = jnp.bitwise_and(jnp.right_shift(words, row // BAND), 1).astype(jnp.float32)
             high, low = split2(value * bit)
-            blocks_ref[slot, row : row + BAND, :] = high
-            blocks_ref[slot, TILE + row : TILE + row + BAND, :] = low
-
-        for p in range(POINTS - 1):
-            fill(r, CHUNKS, p + 1)
-            for c in range(CHUNKS):
-                fill(r, c, p + 1)
-                combine(p, c, finish)
+            block[spot, row : row + BAND, :] = high
+            block[spot, TILE + row : TILE + row + BAND, :] = low
+
+        fill(r, CHUNKS, 1)
+        for c in range(CHUNKS):
+            fill(r, c, 1)
+            combine(0, c, finish)
         load_features(later)
         fill(later_r, CHUNKS, 0)
         for c in range(CHUNKS):
-            combine(POINTS - 1, c, finish)
+            combine(1, c, finish)
             face(later_r, c)
             fill(later_r, c, 0)
+        stored(slot, spot).start()
         high, low = split2(packed[d, :hours, where])
         left = jnp.concatenate([high, low, jnp.ones_like(high)], axis=0)
         acc[r] += jnp.dot(
             jnp.concatenate([left, left], axis=1),
-            blocks_ref[slot],
+            block[spot],
             preferred_element_type=jnp.float32,
         )
         return carry
 
     lax.fori_loop(0, count, one, 0)
+    for spot in range(2):
+
+        @pl.when(count > spot)
+        def _():
+            stored(0, spot).wait()
+
     for r in range(own_tiles):
         lanes = slice(r * TILE, (r + 1) * TILE)
         sums = acc[r, 2 * hours : 2 * hours + 1, :]
@@ -319,10 +340,27 @@
         field_ref[:, lanes] = emi_own[:, lanes] + scale * irr
 
 
-def later_kernel(src_ref, blocks_ref, field_all, emi_own, scale_ref, out_ref, acc):
+def later_kernel(src_ref, blocks_ref, field_all, emi_own, scale_ref, out_ref, acc, held, arrived):
     slots = field_all.shape[0]
     own_tiles = emi_own.shape[1] // TILE
     hours = emi_own.shape[0]
+
+    def fetch(slot):
+        return pltpu.make_async_copy(blocks_ref.at[slot], held.at[slot], arrived.at[slot])
+
+    for r in range(own_tiles):
+
+        def begin(d, carry):
+            slot = d * own_tiles + r
+
+            @pl.when(src_ref[slot, 0] >= 0)
+            def _():
+                fetch(slot).start()
+
+            return carry
+
+        lax.fori_loop(0, slots, begin, 0)
+
     for r in range(own_tiles):
         lanes = slice(r * TILE, (r + 1) * TILE)
         acc[...] = jnp.zeros_like(acc)
@@ -336,9 +374,10 @@
                 where = pl.ds(pl.multiple_of(src * TILE, TILE), TILE)
                 high, low = split2(field_all[d, :, where])
                 left = jnp.concatenate([high, low], axis=0)
+                fetch(slot).wait()
                 acc[...] += jnp.dot(
                     jnp.concatenate([left, left], axis=1),
-                    blocks_ref[slot],
+                    held[slot],
                     preferred_element_type=jnp.float32,
                 )
 
@@ -388,15 +427,17 @@
             jax.ShapeDtypeStruct((1, width), f32),
         ),
         in_specs=[SMEM] + [VMEM] * 5,
-        out_specs=(VMEM,) * 4,
+        out_specs=(ANY,) + (VMEM,) * 3,
         scratch_shapes=[
             pltpu.SMEM((tiles,), jnp.int32),
             pltpu.VMEM((own_tiles, FEATS, SPAN), jnp.bfloat16),
             pltpu.VMEM((SPAN, FEATS), jnp.bfloat16),
-            pltpu.VMEM((2, SPAN, TILE), f32),
+            pltpu.VMEM((2, SPAN, WIDE), f32),
             pltpu.VMEM((POINTS * TILE, TILE), f32),
             pltpu.VMEM((TILE, TILE), f32),
             pltpu.VMEM((own_tiles, 3 * hours, TILE), f32),
+            pltpu.VMEM((2, 2 * TILE, TILE), jnp.bfloat16),
+            dma((2,)),
         ],
         compiler_params=limit,
     )(codes, packed, listed, geometry, emission, reflect.reshape(1, width))
@@ -414,9 +455,13 @@
     radiosity = pl.pallas_call(
         later_kernel,
         out_shape=jax.ShapeDtypeStruct((hours, width), f32),
-        in_specs=[SMEM] + [VMEM] * 4,
+        in_specs=[SMEM, ANY] + [VMEM] * 3,
         out_specs=VMEM,
-        scratch_shapes=[pltpu.VMEM((2 * hours, TILE), f32)],
+        scratch_shapes=[
+            pltpu.VMEM((2 * hours, TILE), f32),
+            pltpu.VMEM((tiles, 2 * TILE, TILE), jnp.bfloat16),
+            dma((tiles,)),
+        ],
         compiler_params=limit,
     )(codes, blocks, field_all, emission, scale)
     return (radiosity, sums.reshape(width))

time: 69.6 us -> 69.7 us (level); the launches traced: 70.4 us -> 69.3 us
  Pallas kernels: 69.1 us -> 68 us
    pallas_call x1, Pallas kernels: 17.2 us -> 18.9 us  [on_device(): pl.pallas_call(functools.partial(field_kernel, n), out_shape=jax.ShapeDty...]
    pallas_call x1, Pallas kernels: 23.9 us -> 22.5 us  [on_device(): pl.pallas_call(first_kernel, out_shape=(jax.ShapeDtypeStruct((tiles, 2 *...]
    pallas_call x1, Pallas kernels: 6.6 us -> 5.27 us  [on_device(): pl.pallas_call(later_kernel, out_shape=jax.ShapeDtypeStruct((hours, width...]
where the time goes in v1:
time: 69.7 us; the launch traced here: 69.3 us
  Pallas kernels  68 us (98%)
  between operations  1.3 us (2%)
    pallas_call x1, Pallas kernels, on_device(): pl.pallas_call(first_kernel, out_shape=(jax.ShapeDtypeStruct((tiles, 2 *...  22.5 us
    pallas_call x1, Pallas kernels, on_device(): pl.pallas_call(functools.partial(share_kernel, n), out_shape=(jax.ShapeDt...  19.7 us
    pallas_call x1, Pallas kernels, on_device(): pl.pallas_call(functools.partial(field_kernel, n), out_shape=jax.ShapeDty...  18.9 us
    pallas_call x1, Pallas kernels, on_device(): pl.pallas_call(later_kernel, out_shape=jax.ShapeDtypeStruct((hours, width...  5.27 us
    pallas_call x1, Pallas kernels, on_device(): pl.pallas_call(sort_kernel, out_shape=jax.ShapeDtypeStruct((tiles, 1, TIL...  1.64 us

profile of v1, /device:TPU:1, one launch (start us, length us, event | category | flops | bytes accessed | tf_op | source)
XLA Modules:
  0.0 69.3 jit_solution(7410231821448580868)
XLA Ops:
  1.3 1.6 %shard_map.86.table_ref = s32[32,1,384]{2,1,0:T(1,128)} custom-call(s32[32]{0:T(128)} %recv_ref.1, s32[32]{0:T(128)} %src_ref.1, s32[1]{0:T(128)S(6)} %copy.9.count_ref, s32[32,256]{1,0:T(8,128)} %occ_ref.1), custom_call_target="tpu_custom_call" | custom-call | tf_op jit(solution)/shard_map/pallas_call | solution.py:399
  2.9 19.7 %shard_map.87 = (f32[16,32,512]{2,1,0:T(8,128)}, s32[16,2,1,384]{3,2,1,0:T(1,128)}, s32[32,128]{1,0:T(8,128)}) custom-call(f32[16,512]{1,0:T(8,128)} %emi_own.3, f32[9,512]{1,0:T(8,128)} %geo_own.1, s32[32,1,384]{2,1,0:T(1,128)} %shard_map.86.table_ref), custom_call_target="tpu_custom_call" | custom-call | tf_op jit(solution)/shard_map/pallas_call | solution.py:406
  22.6 22.5 %shard_map.88 = (bf16[32,512,256]{2,1,0:T(8,128)(2,1)}, f32[16,512]{1,0:T(8,128)}, f32[1,512]{1,0:T(1,128)}, f32[1,512]{1,0:T(1,128)}) custom-call(s32[32,128]{1,0:T(8,128)} %get-tuple-element.9.src_ref, f32[16,32,512]{2,1,0:T(8,128)} %get-tuple-element.10.packed, s32[16,2,1,384]{3,2,1,0:T(1,128)} %get-tuple-element.11.occ_ref, f32[9,512]{1,0:T(8,128)} %geo_own.1, ...), custom_call_target="tpu_custom_call" | custom-call | tf_op jit(solution)/shard_map/pallas_call | solution.py:421
  45.1 18.9 %shard_map.89.field_all = f32[16,16,512]{2,1,0:T(8,128)} custom-call(f32[16,512]{1,0:T(8,128)} %get-tuple-element.13.field_ref), custom_call_target="tpu_custom_call" | custom-call | tf_op jit(solution)/shard_map/pallas_call | solution.py:445
  64.0 5.3 %shard_map.90 = f32[16,512]{1,0:T(8,128)} custom-call(s32[32,128]{1,0:T(8,128)} %get-tuple-element.9.src_ref, bf16[32,512,256]{2,1,0:T(8,128)(2,1)} %get-tuple-element.12.blocks_ref, f32[16,16,512]{2,1,0:T(8,128)} %shard_map.89.field_all, f32[16,512]{1,0:T(8,128)} %emi_own.3, f32[1,512]{1,0:T(1,128)} %get-tuple-element.14.scale_ref), custom_call_target="tpu_custom_call" | custom-call | tf_op jit(solution)/shard_map/pallas_call | solution.py:455

commit v2 on v1

--- a/solution.py
+++ b/solution.py
@@ -13,7 +13,7 @@
 BAND = TILE // GROUPS
 POINTS = 4
 FEATS = 48
-PACK = 32
+LANES = 128
 CHUNKS = 4
 PART = TILE // CHUNKS
 WIDE = 2 * TILE
@@ -98,28 +98,35 @@
     return 3 * depth - 1 + 2 * depth
 
 
-def greet(n):
-    me = lax.axis_index("row")
+def greet(devices):
     barrier = pltpu.get_barrier_semaphore()
-    for step in range(1, n):
+    for device in devices:
         pl.semaphore_signal(
             barrier,
             inc=1,
-            device_id={"row": lax.rem(me + step, n)},
+            device_id={"row": device},
             device_id_type=pl.DeviceIdType.MESH,
         )
-    pl.semaphore_wait(barrier, n - 1)
+    pl.semaphore_wait(barrier, len(devices))
 
 
 def share_kernel(n, emi_ref, geo_ref, table_ref, out_ref, listed_ref, codes_ref, send, recv, list_send, list_recv):
     me = lax.axis_index("row")
     hours = emi_ref.shape[0]
     own_tiles = table_ref.shape[0] // n
-    out_ref[me, :hours] = emi_ref[...]
-    out_ref[me, hours : hours + 9] = geo_ref[...]
-    out_ref[me, hours + 9 :] = jnp.zeros_like(out_ref[me, hours + 9 :])
+    blocks = emi_ref.shape[1] // LANES
+    for k in range(blocks):
+        lanes = slice(k * LANES, (k + 1) * LANES)
+        out_ref[me, k * hours : (k + 1) * hours] = emi_ref[:, lanes]
+        row = blocks * hours + k * 8
+        out_ref[me, row : row + 8] = geo_ref[0:8, lanes]
+        row = blocks * (hours + 8) + k
+        out_ref[me, row : row + 1] = geo_ref[8:9, lanes]
+    used = blocks * (hours + 9)
+    if used < out_ref.shape[1]:
+        out_ref[me, used:] = jnp.zeros((out_ref.shape[1] - used, LANES), jnp.float32)
     listed_ref[me] = table_ref[pl.ds(me * own_tiles, own_tiles)]
-    greet(n)
+    greet([lax.rem(me + step, n) for step in range(1, n)])
     finish = start_gather(n, out_ref.at[me], out_ref, send, recv)
     lists = []
     for step in range(1, n):
@@ -144,7 +151,12 @@
 def field_kernel(n, field_ref, out_ref, send, recv):
     me = lax.axis_index("row")
     out_ref[me] = field_ref[...]
-    greet(n)
+    core = lax.rem(me, 2)
+    side = lax.rem(me // 2, 2)
+    greet(
+        [lax.rem(me + 4 * step, n) for step in range(1, n // 4)]
+        + [me + 2 - 4 * side, me + 1 - 2 * core]
+    )
     start_gather(n, field_ref, out_ref, send, recv)()
 
 
@@ -209,6 +221,7 @@
     own_tiles = geo_own.shape[1] // TILE
     slots = packed.shape[0] * own_tiles
     hours = emi_own.shape[0]
+    blocks = geo_own.shape[1] // LANES
     center = jnp.mean(geo_own[0:3, :], axis=1, keepdims=True)
 
     def listing(k, live):
@@ -221,12 +234,27 @@
     acc[...] = jnp.zeros_like(acc)
 
     def place(slot):
-        src = jnp.maximum(src_ref[slot, 0], 0)
-        return slot // own_tiles, pl.ds(pl.multiple_of(src * TILE, TILE), TILE)
+        return slot // own_tiles, jnp.maximum(src_ref[slot, 0], 0) * (TILE // LANES)
+
+    def emission_of(d, first):
+        rows = [pl.multiple_of((first + k) * hours, 8) for k in range(TILE // LANES)]
+        return jnp.concatenate([packed[d, pl.ds(row, hours), :] for row in rows], axis=1)
+
+    def geometry_of(d, first):
+        halves = []
+        for k in range(TILE // LANES):
+            row = pl.multiple_of(blocks * hours + (first + k) * 8, 8)
+            last = blocks * (hours + 8) + first + k
+            halves.append(
+                jnp.concatenate(
+                    [packed[d, pl.ds(row, 8), :], packed[d, pl.ds(last, 1), :]], axis=0
+                )
+            )
+        return jnp.concatenate(halves, axis=1)
 
     def load_features(slot):
-        d, where = place(slot)
-        rows = source_features(packed[d, hours : hours + 9, where], center)
+        d, first = place(slot)
+        rows = source_features(geometry_of(d, first), center)
         for c in range(CHUNKS):
             for q in range(POINTS):
                 src_feat[c * TILE + q * PART : c * TILE + (q + 1) * PART, :] = rows[
@@ -289,7 +317,7 @@
         later = order[jnp.minimum(i + 1, count - 1)]
         r = lax.rem(slot, own_tiles)
         later_r = lax.rem(later, own_tiles)
-        d, where = place(slot)
+        d, first = place(slot)
         words = occ_ref[d, r, :, :TILE]
         spot = lax.rem(i, 2)
 
@@ -314,7 +342,7 @@
             face(later_r, c)
             fill(later_r, c, 0)
         stored(slot, spot).start()
-        high, low = split2(packed[d, :hours, where])
+        high, low = split2(emission_of(d, first))
         left = jnp.concatenate([high, low, jnp.ones_like(high)], axis=0)
         acc[r] += jnp.dot(
             jnp.concatenate([left, left], axis=1),
@@ -406,7 +434,7 @@
     packed, listed, codes = pl.pallas_call(
         functools.partial(share_kernel, n),
         out_shape=(
-            jax.ShapeDtypeStruct((n, PACK, width), f32),
+            jax.ShapeDtypeStruct((n, -(-(width // LANES) * (hours + 9) // 8) * 8, LANES), f32),
             jax.ShapeDtypeStruct((n, own_tiles, 1, TILE + 128), jnp.int32),
             jax.ShapeDtypeStruct((tiles, 128), jnp.int32),
         ),

time: 69.7 us -> 65.9 us (0.945)
  Pallas kernels: 68 us -> 64.8 us
    pallas_call x1, Pallas kernels: 18.9 us -> 17.2 us  [on_device(): pl.pallas_call(functools.partial(field_kernel, n), out_shape=jax.ShapeDty...]
    pallas_call x1, Pallas kernels: 19.7 us -> 18.4 us  [on_device(): pl.pallas_call(functools.partial(share_kernel, n), out_shape=(jax.ShapeDt...]
where the time goes in v2:
time: 65.9 us; the launch traced here: 66.1 us
  Pallas kernels  64.8 us (98%)
  between operations  1.3 us (2%)
    pallas_call x1, Pallas kernels, on_device(): pl.pallas_call(first_kernel, out_shape=(jax.ShapeDtypeStruct((tiles, 2 *...  22.4 us
    pallas_call x1, Pallas kernels, on_device(): pl.pallas_call(functools.partial(share_kernel, n), out_shape=(jax.ShapeDt...  18.4 us
    pallas_call x1, Pallas kernels, on_device(): pl.pallas_call(functools.partial(field_kernel, n), out_shape=jax.ShapeDty...  17.2 us
    pallas_call x1, Pallas kernels, on_device(): pl.pallas_call(later_kernel, out_shape=jax.ShapeDtypeStruct((hours, width...  5.27 us
    pallas_call x1, Pallas kernels, on_device(): pl.pallas_call(sort_kernel, out_shape=jax.ShapeDtypeStruct((tiles, 1, TIL...  1.47 us

profile of v2, /device:TPU:1, one launch (start us, length us, event | category | flops | bytes accessed | tf_op | source)
XLA Modules:
  0.0 66.1 jit_solution(9149172931322676188)
XLA Ops:
  1.3 1.5 %shard_map.86.table_ref = s32[32,1,384]{2,1,0:T(1,128)} custom-call(s32[32]{0:T(128)} %recv_ref.1, s32[32]{0:T(128)} %src_ref.1, s32[1]{0:T(128)S(6)} %copy.9.count_ref, s32[32,256]{1,0:T(8,128)} %occ_ref.1), custom_call_target="tpu_custom_call" | custom-call | tf_op jit(solution)/shard_map/pallas_call | solution.py:427
  2.8 18.4 %shard_map.87 = (f32[16,104,128]{2,1,0:T(8,128)}, s32[16,2,1,384]{3,2,1,0:T(1,128)}, s32[32,128]{1,0:T(8,128)}) custom-call(f32[16,512]{1,0:T(8,128)} %emi_own.3, f32[9,512]{1,0:T(8,128)} %geo_own.1, s32[32,1,384]{2,1,0:T(1,128)} %shard_map.86.table_ref), custom_call_target="tpu_custom_call" | custom-call | tf_op jit(solution)/shard_map/pallas_call | solution.py:434
  21.1 22.4 %shard_map.88 = (bf16[32,512,256]{2,1,0:T(8,128)(2,1)}, f32[16,512]{1,0:T(8,128)}, f32[1,512]{1,0:T(1,128)}, f32[1,512]{1,0:T(1,128)}) custom-call(s32[32,128]{1,0:T(8,128)} %get-tuple-element.9.src_ref, f32[16,104,128]{2,1,0:T(8,128)} %get-tuple-element.10.packed, s32[16,2,1,384]{3,2,1,0:T(1,128)} %get-tuple-element.11.occ_ref, f32[9,512]{1,0:T(8,128)} %geo_own.1, ...), custom_call_target="tpu_custom_call" | custom-call | tf_op jit(solution)/shard_map/pallas_call | solution.py:449
  43.5 17.2 %shard_map.89.field_all = f32[16,16,512]{2,1,0:T(8,128)} custom-call(f32[16,512]{1,0:T(8,128)} %get-tuple-element.13.field_ref), custom_call_target="tpu_custom_call" | custom-call | tf_op jit(solution)/shard_map/pallas_call | solution.py:473
  60.8 5.3 %shard_map.90 = f32[16,512]{1,0:T(8,128)} custom-call(s32[32,128]{1,0:T(8,128)} %get-tuple-element.9.src_ref, bf16[32,512,256]{2,1,0:T(8,128)(2,1)} %get-tuple-element.12.blocks_ref, f32[16,16,512]{2,1,0:T(8,128)} %shard_map.89.field_all, f32[16,512]{1,0:T(8,128)} %emi_own.3, f32[1,512]{1,0:T(1,128)} %get-tuple-element.14.scale_ref), custom_call_target="tpu_custom_call" | custom-call | tf_op jit(solution)/shard_map/pallas_call | solution.py:483
